TPU v7x, 32 devices: a whole 2x2x4 slice. The times are simulated.
32 devices in a mesh: section: 2 (over core), dp: 8 (over z, x), fsdp: 2 (over y).
Axes of the slice: x: 2, y: 2, z: 4, core: 2. Of those that a mesh axis runs over, the one named last changes fastest.
Arguments:
- images: bfloat16 [96, 196, 512], P(('dp', 'fsdp')), may hold values from -6 to 6
- out_grad: bfloat16 [96, 196, 512], P(('dp', 'fsdp')), may hold values from -6 to 6
- live: int32 [16, 2], P(('dp', 'fsdp')), may hold values from 0 to 3, as said below
- qkv_w: bfloat16 [2, 512, 1536], P('section', 'fsdp'), may hold values from -0.25 to 0.25
- proj_w: bfloat16 [2, 512, 512], P('section', 'fsdp'), may hold values from -0.75 to 0.75
- fc1_w: bfloat16 [2, 512, 2048], P('section', 'fsdp'), may hold values from -0.25 to 0.25
- fc2_w: bfloat16 [2, 2048, 512], P('section', 'fsdp'), may hold values from -0.125 to 0.125
- gains: bfloat16 [2, 2, 512], P('section', None, 'fsdp'), may hold values from 0.5 to 1.5
- biases: bfloat16 [2, 6, 512], P('section', None, 'fsdp'), may hold values from -1.796875 to 1.796875
- hidden_bias: bfloat16 [2, 2048], P('section', 'fsdp'), may hold values from -1.796875 to 1.796875
- table: float32 [2, 169, 16], P('section'), may hold values from -6 to 6
- rel_index: int32 [49, 49], replicated, may hold values from 0 to 168
- region: int32 [196], replicated, may hold values from 0 to 3
Outputs:
- layer_out: bfloat16 [2, 96, 196, 512], P('section', ('dp', 'fsdp'))
- input_grad: bfloat16 [2, 96, 196, 512], P('section', ('dp', 'fsdp'))
- d_qkv_w: float32 [2, 512, 1536], P('section', 'fsdp')
- d_proj_w: float32 [2, 512, 512], P('section', 'fsdp')
- d_fc1_w: float32 [2, 512, 2048], P('section', 'fsdp')
- d_fc2_w: float32 [2, 2048, 512], P('section', 'fsdp')
- d_gains: float32 [2, 2, 512], P('section', None, 'fsdp')
- d_biases: float32 [2, 6, 512], P('section', None, 'fsdp')
- d_hidden_bias: float32 [2, 2048], P('section', 'fsdp')
- d_table: float32 [2, 169, 16], P('section')
- d_query_bias: float32 [2, 512], P('section', 'fsdp')
Inputs may be any that keep to these rules, and one draw needn't show every extreme that they name: The first live[s, m] of the 3 slots of micro-batch m of shard s are live; in every draw some shard has all 3 live in some micro-batch.
All inputs are finite; a program needn't handle non-finite values.
Results may differ from a plain program's by a relative error of at most 0.018.
Values may be sent and summed in bfloat16 or wider, within the bound.
A program may use at most 256 MiB of HBM per device.

v0:
```python
import jax
import jax.numpy as jnp
from jax import lax
from jax.sharding import PartitionSpec as P

D = 512
HEADS = 16
HEAD_DIM = 32
GRID = 14
WIN = 7
TOK = 196
WTOK = 49
NWIN = 4
TABLE = 169
MB = 2


EPS = 1e-05
HIGH = lax.Precision.HIGHEST


def shifted(block, axis, distance):
    devices = range(lax.axis_size(axis))
    route = [(i - distance, i) for i in devices if i - distance in devices]
    return lax.ppermute(block, axis, route)


def norm(values, gain, offset):
    middle = jnp.mean(values, -1, keepdims=True)
    centred = values - middle
    spread = jnp.mean(centred * centred, -1, keepdims=True)
    return centred * lax.rsqrt(spread + EPS) * gain + offset


def to_windows(grid):
    batch, side, _, depth = grid.shape
    across = side // WIN
    tiles = grid.reshape(batch, across, WIN, across, WIN, depth).transpose(0, 1, 3, 2, 4, 5)
    return tiles.reshape(batch, across * across, WIN * WIN, depth)


def from_windows(tiles):
    batch, _, _, depth = tiles.shape
    across = GRID // WIN
    grid = tiles.reshape(batch, across, across, WIN, WIN, depth).transpose(0, 1, 3, 2, 4, 5)
    return grid.reshape(batch, GRID, GRID, depth)


def rolled(grid, amount, flag):
    return lax.cond(
        flag, lambda field: jnp.roll(field, (amount, amount), (1, 2)), lambda field: field, grid
    )


def pick(flag, first, second):
    return lax.cond(flag, lambda one, two: one, lambda one, two: two, first, second)


def layer_forward(source, weights, flag, rel_bias, mask_add):
    qkv_w, proj_w, fc1_w, fc2_w, gains, biases, hidden_bias = weights
    batch = source.shape[0]
    gain_vals = gains.astype(jnp.float32)
    bias_vals = biases.astype(jnp.float32)
    hidden_vals = hidden_bias.astype(jnp.float32)
    normed = norm(source, gain_vals[0], bias_vals[0]).astype(jnp.bfloat16)
    grid = rolled(normed.reshape(batch, GRID, GRID, D), -(WIN // 2), flag)
    windows = to_windows(grid).reshape(-1, D)
    qkv_bias = jnp.concatenate([bias_vals[1], jnp.zeros_like(bias_vals[1]), bias_vals[2]])
    packed = (jnp.dot(windows, qkv_w, preferred_element_type=jnp.float32) + qkv_bias).astype(
        jnp.bfloat16
    )
    head_shape = (batch, NWIN, WTOK, HEADS, HEAD_DIM)
    query = packed[:, :D].reshape(head_shape)
    keys = packed[:, D : 2 * D].reshape(head_shape)
    values = packed[:, 2 * D :].reshape(head_shape)
    scores = jnp.einsum(
        "bwqhd,bwkhd->bwhqk", query, keys, preferred_element_type=jnp.float32
    ) * HEAD_DIM ** (-0.5)
    scores = scores + rel_bias[None, None] + mask_add[None, :, None]
    peak = jnp.max(scores, -1, keepdims=True)
    raised = jnp.exp(scores - peak)
    probs = raised / jnp.sum(raised, -1, keepdims=True)
    low_probs = probs.astype(jnp.bfloat16)
    mixed = jnp.einsum("bwhqk,bwkhd->bwqhd", low_probs, values, preferred_element_type=jnp.float32)
    mixed = mixed.astype(jnp.bfloat16).reshape(-1, D)
    projected = jnp.dot(mixed, proj_w, preferred_element_type=jnp.float32) + bias_vals[3]
    back = rolled(from_windows(projected.reshape(batch, NWIN, WTOK, D)), WIN // 2, flag)
    middle = source + back.reshape(batch, TOK, D)
    normed_two = norm(middle, gain_vals[1], bias_vals[4]).astype(jnp.bfloat16).reshape(-1, D)
    hidden = jnp.dot(normed_two, fc1_w, preferred_element_type=jnp.float32) + hidden_vals
    active = jax.nn.gelu(hidden, approximate=False).astype(jnp.bfloat16)
    output = middle + (
        jnp.dot(active, fc2_w, preferred_element_type=jnp.float32) + bias_vals[5]
    ).reshape(batch, TOK, D)
    saved = (
        windows,
        query,
        keys,
        values,
        probs,
        low_probs,
        mixed,
        middle,
        normed_two,
        hidden,
        active,
    )
    return (output, saved)


def layer_backward(source, upstream, weights, flag, rel_bias, mask_add, onehot):
    qkv_w, proj_w, fc1_w, fc2_w, gains, biases, hidden_bias = weights
    gain_vals = gains.astype(jnp.float32)
    bias_vals = biases.astype(jnp.float32)
    batch = source.shape[0]
    _, saved = layer_forward(source, weights, flag, rel_bias, mask_add)
    windows, query, keys, values, probs, low_probs, mixed, middle, normed_two, hidden, active = (
        saved
    )
    up_rows = upstream.reshape(-1, D)
    up_low = up_rows.astype(jnp.bfloat16)
    d_fc2 = jnp.einsum("rf,rd->fd", active, up_low, preferred_element_type=jnp.float32)
    d_out_bias = jnp.sum(up_rows, 0)
    d_active = jnp.einsum("rd,fd->rf", up_low, fc2_w, preferred_element_type=jnp.float32)
    _, gelu_back = jax.vjp(lambda point: jax.nn.gelu(point, approximate=False), hidden)
    d_hidden = gelu_back(d_active)[0].astype(jnp.bfloat16)
    d_fc1 = jnp.einsum("rc,rf->cf", normed_two, d_hidden, preferred_element_type=jnp.float32)
    d_hidden_bias = jnp.sum(d_hidden.astype(jnp.float32), 0)
    d_normed_two = jnp.einsum("rf,cf->rc", d_hidden, fc1_w, preferred_element_type=jnp.float32)
    _, norm_two_back = jax.vjp(norm, middle.reshape(-1, D), gain_vals[1], bias_vals[4])
    d_middle_norm, d_gain_two, d_shift_two = norm_two_back(d_normed_two)
    d_middle = up_rows + d_middle_norm
    d_grid = rolled(d_middle.reshape(batch, GRID, GRID, D), -(WIN // 2), flag)
    d_projected = to_windows(d_grid).reshape(-1, D).astype(jnp.bfloat16)
    d_proj = jnp.einsum("rc,rd->cd", mixed, d_projected, preferred_element_type=jnp.float32)
    d_proj_bias = jnp.sum(d_projected.astype(jnp.float32), 0)
    d_mixed = jnp.einsum("rd,cd->rc", d_projected, proj_w, preferred_element_type=jnp.float32)
    d_mixed = d_mixed.astype(jnp.bfloat16).reshape(batch, NWIN, WTOK, HEADS, HEAD_DIM)
    d_probs = jnp.einsum("bwqhd,bwkhd->bwhqk", d_mixed, values, preferred_element_type=jnp.float32)
    d_values = jnp.einsum(
        "bwhqk,bwqhd->bwkhd", low_probs, d_mixed, preferred_element_type=jnp.float32
    )
    d_scores = probs * (d_probs - jnp.sum(probs * d_probs, -1, keepdims=True))
    d_scores = d_scores.astype(jnp.bfloat16)
    d_rel = jnp.sum(d_scores.astype(jnp.float32), (0, 1))
    d_table = jnp.einsum("pt,hp->th", onehot, d_rel.reshape(HEADS, -1), precision=HIGH)
    d_query = jnp.einsum(
        "bwhqk,bwkhd->bwqhd", d_scores, keys, preferred_element_type=jnp.float32
    ) * HEAD_DIM ** (-0.5)
    d_keys = jnp.einsum(
        "bwhqk,bwqhd->bwkhd", d_scores, query, preferred_element_type=jnp.float32
    ) * HEAD_DIM ** (-0.5)
    low_query = d_query.reshape(-1, D).astype(jnp.bfloat16)
    low_keys = d_keys.reshape(-1, D).astype(jnp.bfloat16)
    low_values = d_values.reshape(-1, D).astype(jnp.bfloat16)
    d_qkv = jnp.concatenate(
        [
            jnp.einsum("rc,re->ce", windows, low_query, preferred_element_type=jnp.float32),
            jnp.einsum("rc,re->ce", windows, low_keys, preferred_element_type=jnp.float32),
            jnp.einsum("rc,re->ce", windows, low_values, preferred_element_type=jnp.float32),
        ],
        axis=1,
    )
    d_query_bias = jnp.sum(low_query.astype(jnp.float32), 0)
    d_value_bias = jnp.sum(low_values.astype(jnp.float32), 0)
    d_windows = jnp.einsum("re,ce->rc", low_query, qkv_w[:, :D], preferred_element_type=jnp.float32)
    d_windows = d_windows + jnp.einsum(
        "re,ce->rc", low_keys, qkv_w[:, D : 2 * D], preferred_element_type=jnp.float32
    )
    d_windows = d_windows + jnp.einsum(
        "re,ce->rc", low_values, qkv_w[:, 2 * D :], preferred_element_type=jnp.float32
    )
    d_normed = rolled(
        from_windows(d_windows.reshape(batch, NWIN, WTOK, D)), WIN // 2, flag
    ).reshape(-1, D)
    _, norm_one_back = jax.vjp(norm, source.reshape(-1, D), gain_vals[0], bias_vals[0])
    d_source_norm, d_gain_one, d_shift_one = norm_one_back(d_normed)
    d_source = (d_middle + d_source_norm).reshape(batch, TOK, D)
    d_gains = jnp.stack([d_gain_one, d_gain_two])
    d_biases = jnp.stack(
        [d_shift_one, d_query_bias, d_value_bias, d_proj_bias, d_shift_two, d_out_bias]
    )
    return (d_source, (d_qkv, d_proj, d_fc1, d_fc2, d_gains, d_biases, d_hidden_bias, d_table))


def spread_rows(grad, axis_pos, wide, deep):
    shape = grad.shape
    length = shape[axis_pos]
    split = grad.reshape(
        shape[:axis_pos] + (wide, deep, length // (wide * deep)) + shape[axis_pos + 1 :]
    )
    return jnp.swapaxes(split, axis_pos, axis_pos + 1).reshape(shape)


def body(
    images,
    out_grad,
    live,
    qkv_w,
    proj_w,
    fc1_w,
    fc2_w,
    gains,
    biases,
    hidden_bias,
    table,
    rel_index,
    region,
):
    section = lax.axis_index("section")
    flag = section == 1
    gathered = (
        lax.all_gather(qkv_w, "fsdp", axis=1, tiled=True),
        lax.all_gather(proj_w, "fsdp", axis=1, tiled=True),
        lax.all_gather(fc1_w, "fsdp", axis=1, tiled=True),
        lax.all_gather(fc2_w, "fsdp", axis=1, tiled=True),
        lax.all_gather(gains, "fsdp", axis=2, tiled=True),
        lax.all_gather(biases, "fsdp", axis=2, tiled=True),
        lax.all_gather(hidden_bias, "fsdp", axis=1, tiled=True),
    )
    weights = tuple((piece[0] for piece in gathered))
    onehot = (rel_index.reshape(-1)[:, None] == jnp.arange(TABLE, dtype=jnp.int32)[None, :]).astype(
        jnp.float32
    )
    rel_bias = jnp.dot(onehot, table[0], precision=HIGH).T.reshape(HEADS, WTOK, WTOK)
    region_win = to_windows(region.reshape(1, GRID, GRID, 1)).reshape(NWIN, WTOK)
    differs = region_win[:, :, None] != region_win[:, None, :]
    mask_add = jnp.where(flag & differs, -100.0, 0.0).astype(jnp.float32)
    per_batch = images.shape[0] // MB
    own_inputs = images.reshape(MB, per_batch, TOK, D)
    slots = jnp.arange(per_batch, dtype=jnp.int32)
    keep = slots[None, :] < live[0][:, None]
    cotangent = jnp.where(
        keep[:, :, None, None], out_grad.reshape(MB, per_batch, TOK, D), jnp.zeros((), jnp.bfloat16)
    )
    inbox = jnp.zeros((per_batch, TOK, D), jnp.bfloat16)
    kept_inputs = jnp.zeros((MB + 1, per_batch, TOK, D), jnp.float32)
    outputs = jnp.zeros((MB + 1, per_batch, TOK, D), jnp.bfloat16)
    for moment in range(MB + 1):
        position = moment - section
        valid = (position >= 0) & (position < MB)
        which = jnp.clip(position, 0, MB - 1)
        slot = jnp.where(valid, position, MB)
        own = lax.dynamic_index_in_dim(own_inputs, which, 0, keepdims=False)
        source = pick(flag, inbox, own).astype(jnp.float32)
        result, _ = layer_forward(source, weights, flag, rel_bias, mask_add)
        result_low = result.astype(jnp.bfloat16)
        kept_inputs = lax.dynamic_update_index_in_dim(kept_inputs, source, slot, 0)
        outputs = lax.dynamic_update_index_in_dim(outputs, result_low, slot, 0)
        if moment < MB:
            inbox = shifted(result_low, "section", 1)
    grad_inbox = jnp.zeros((per_batch, TOK, D), jnp.bfloat16)
    source_grads = jnp.zeros((MB + 1, per_batch, TOK, D), jnp.bfloat16)
    totals = None
    for moment in range(MB + 1):
        position = moment - (1 - section)
        valid = (position >= 0) & (position < MB)
        which = jnp.clip(position, 0, MB - 1)
        slot = jnp.where(valid, position, MB)
        mine = lax.dynamic_index_in_dim(cotangent, which, 0, keepdims=False)
        upstream = pick(flag, mine, grad_inbox).astype(jnp.float32)
        source = lax.dynamic_index_in_dim(kept_inputs, which, 0, keepdims=False)
        d_source, layer_grads = layer_backward(
            source, upstream, weights, flag, rel_bias, mask_add, onehot
        )
        factor = valid.astype(jnp.float32)
        masked = tuple((g * factor for g in layer_grads))
        totals = masked if totals is None else tuple((a + b for a, b in zip(totals, masked)))
        d_low = d_source.astype(jnp.bfloat16)
        source_grads = lax.dynamic_update_index_in_dim(source_grads, d_low, slot, 0)
        if moment < MB:
            grad_inbox = shifted(d_low, "section", -1)
    g_qkv, g_proj, g_fc1, g_fc2, g_gains, g_biases, g_hidden, g_table = totals
    wide = lax.axis_size("fsdp")
    deep = lax.axis_size("dp")
    s_qkv = spread_rows(g_qkv, 0, wide, deep)
    s_proj = spread_rows(g_proj, 0, wide, deep)
    s_fc1 = spread_rows(g_fc1, 0, wide, deep)
    s_fc2 = spread_rows(g_fc2, 0, wide, deep)
    s_gains = spread_rows(g_gains, 1, wide, deep)
    s_biases = spread_rows(g_biases, 1, wide, deep)
    s_hidden = spread_rows(g_hidden, 0, wide, deep)
    pieces = (
        lax.psum_scatter(s_qkv, ("dp", "fsdp"), scatter_dimension=0, tiled=True),
        lax.psum_scatter(s_proj, ("dp", "fsdp"), scatter_dimension=0, tiled=True),
        lax.psum_scatter(s_fc1, ("dp", "fsdp"), scatter_dimension=0, tiled=True),
        lax.psum_scatter(s_fc2, ("dp", "fsdp"), scatter_dimension=0, tiled=True),
        lax.psum_scatter(s_gains, ("dp", "fsdp"), scatter_dimension=1, tiled=True),
        lax.psum_scatter(s_biases, ("dp", "fsdp"), scatter_dimension=1, tiled=True),
        lax.psum_scatter(s_hidden, ("dp", "fsdp"), scatter_dimension=0, tiled=True),
    )
    p_qkv, p_proj, p_fc1, p_fc2, p_gains, p_biases, p_hidden = pieces
    owned = (
        lax.all_gather(p_qkv.astype(jnp.bfloat16), "dp", axis=0, tiled=True).astype(p_qkv.dtype),
        lax.all_gather(p_proj.astype(jnp.bfloat16), "dp", axis=0, tiled=True).astype(p_proj.dtype),
        lax.all_gather(p_fc1.astype(jnp.bfloat16), "dp", axis=0, tiled=True).astype(p_fc1.dtype),
        lax.all_gather(p_fc2.astype(jnp.bfloat16), "dp", axis=0, tiled=True).astype(p_fc2.dtype),
        lax.all_gather(p_gains.astype(jnp.bfloat16), "dp", axis=1, tiled=True).astype(
            p_gains.dtype
        ),
        lax.all_gather(p_biases.astype(jnp.bfloat16), "dp", axis=1, tiled=True).astype(
            p_biases.dtype
        ),
        lax.all_gather(p_hidden.astype(jnp.bfloat16), "dp", axis=0, tiled=True).astype(
            p_hidden.dtype
        ),
    )
    table_total = lax.psum(g_table, ("dp", "fsdp"))
    o_qkv, o_proj, o_fc1, o_fc2, o_gains, o_biases, o_hidden = owned
    layer_out = outputs[:MB].reshape(1, MB * per_batch, TOK, D)
    input_grad = source_grads[:MB].reshape(1, MB * per_batch, TOK, D)
    return (
        layer_out,
        input_grad,
        o_qkv[None],
        o_proj[None],
        o_fc1[None],
        o_fc2[None],
        o_gains[None],
        o_biases[None],
        o_hidden[None],
        table_total[None],
        o_biases[1][None],
    )


def solution(mesh):
    return jax.shard_map(
        body,
        mesh=mesh,
        in_specs=(
            P(("dp", "fsdp"), None, None),
            P(("dp", "fsdp"), None, None),
            P(("dp", "fsdp"), None),
            P("section", "fsdp", None),
            P("section", "fsdp", None),
            P("section", "fsdp", None),
            P("section", "fsdp", None),
            P("section", None, "fsdp"),
            P("section", None, "fsdp"),
            P("section", "fsdp"),
            P("section", None, None),
            P(),
            P(),
        ),
        out_specs=(
            P("section", ("dp", "fsdp"), None, None),
            P("section", ("dp", "fsdp"), None, None),
            P("section", "fsdp", None),
            P("section", "fsdp", None),
            P("section", "fsdp", None),
            P("section", "fsdp", None),
            P("section", None, "fsdp"),
            P("section", None, "fsdp"),
            P("section", "fsdp"),
            P("section", None, None),
            P("section", "fsdp"),
        ),
        check_vma=False,
    )
```

profile of v0, /device:TPU:0, one launch (start us, length us, event | category | flops | bytes accessed | tf_op | source)
XLA Modules:
  0.0 1355.8 jit_solution(13336514538675864121)
XLA Ops:
  26.5 14.0 %all_gather.45 = bf16[1,512,512]{2,1,0:T(8,128)(2,1)S(1)} all-gather(bf16[1,256,512]{2,1,0:T(8,128)(2,1)S(1)} %copy-done.114), channel_id=1, replica_groups=mesh['section'=2,'dp'=8,'fsdp'=2] {'fsdp'}, dimensions={1}, use_global_device_ids=true | all-gather | bytes 786432 | tf_op jit(solution)/shard_map/all_gather | solution.py:214
  79.9 34.7 %all-gather.13.cloned.1.call-done = bf16[1,2048,512]{2,1,0:T(8,128)(2,1)} async-done(((bf16[1,1024,512]{2,1,0:T(8,128)(2,1)}), bf16[1,2048,512]{2,1,0:T(8,128)(2,1)}) %all-gather.13.cloned.1.call-update) | async-done | bytes 2097168 | tf_op jit(solution)/shard_map/all_gather | solution.py:216
  114.6 15.4 %fusion.215 = f32[588,512]{1,0:T(8,128)} fusion(bf16[1,2048,512]{2,1,0:T(8,128)(2,1)} %all-gather.13.cloned.1.call-done, bf16[588,512]{1,0:T(8,128)(2,1)S(1)} %reshape.1515, f32[2048]{0:T(1024)S(1)} %bitcast.566, bf16[1,512,2048]{2,1,0:T(8,128)(2,1)} %all-gather.11.cloned.1.call-done, f32[512]{0:T(512)S(1)} %bitcast.605), kind=kOutput, calls=%fused_computation.379 | convolution fusion | flops 2546030592 | bytes 6010880 | tf_op jit(solution)/shard_map/dot_general | solution.py:93
  172.5 15.4 %fusion.208 = f32[588,512]{1,0:T(8,128)} fusion(bf16[1,2048,512]{2,1,0:T(8,128)(2,1)} %all-gather.13.cloned.1.call-done, bf16[588,512]{1,0:T(8,128)(2,1)S(1)} %reshape.1523, f32[2048]{0:T(1024)S(1)} %bitcast.567, bf16[1,512,2048]{2,1,0:T(8,128)(2,1)} %all-gather.11.cloned.1.call-done, f32[512]{0:T(512)S(1)} %bitcast.606), kind=kOutput, calls=%fused_computation.378 | convolution fusion | flops 2546030592 | bytes 6010880 | tf_op jit(solution)/shard_map/dot_general | solution.py:93
  264.8 7.5 fusion.454
  338.7 7.5 fusion.453
  409.5 7.5 fusion.452
  476.7 34.1 %fusion.35 = (f32[588,2048]{1,0:T(8,128)}, f32[588,2048]{1,0:T(8,128)}, f32[588,2048]{1,0:T(8,128)S(1)}, f32[588,2048]{1,0:T(8,128)}) fusion(f32[2048]{0:T(1024)S(1)} %bitcast.568, f32[588,2048]{1,0:T(8,128)S(1)} %fusion.149, f32[588,2048]{1,0:T(8,128)S(1)} %fusion.153, bf16[588,512]{1,0:T(8,128)(2,1)S(1)} %copy-done.106, ...), kind=kOutput, calls=%fused_computation.107 | convolution fusion | flops 1460723712 | bytes 31608832 | tf_op jit(solution)/shard_map/dot_general | solution.py:90
  587.5 7.8 fusion.117
  600.5 7.2 convert_reduce_fusion.4
  673.8 7.7 fusion.118
  687.8 8.8 multiply_add_fusion
  882.0 15.8 %fusion.201 = f32[588,512]{1,0:T(8,128)} fusion(bf16[1,2048,512]{2,1,0:T(8,128)(2,1)} %all-gather.13.cloned.1.call-done, bf16[588,512]{1,0:T(8,128)(2,1)} %reshape.1531, f32[2048]{0:T(1024)S(1)} %bitcast.575, bf16[1,512,2048]{2,1,0:T(8,128)(2,1)} %all-gather.11.cloned.1.call-done, f32[512]{0:T(512)S(1)} %bitcast.607), kind=kOutput, calls=%fused_computation.377 | convolution fusion | flops 2546030592 | bytes 6010880 | tf_op jit(solution)/shard_map/dot_general | solution.py:93
  923.5 76.1 %all-reduce.1 = (bf16[2048]{0:T(1024)(128)(2,1)S(1)}, f32[1,169,16]{1,2,0:T(8,128)}) all-reduce(f32[2048]{0:T(1024)S(1)} %bitcast.598, f32[1,169,16]{1,2,0:T(8,128)S(1)} %fusion.242), channel_id=8, replica_groups=mesh['section'=2,'dp'=8,'fsdp'=2] {'dp','fsdp'}, use_global_device_ids=true, to_apply=%region_141.142.clone | all-reduce | flops 4752 | bytes 33920
  999.6 16.1 %all-gather.2 = bf16[8,1,128]{2,1,0:T(2,128)(2,1)S(1)} all-gather(bf16[1,1,128]{2,1,0:T(2,128)(2,1)S(1)} %fusion.316), channel_id=1, replica_groups=mesh['section'=2,'dp'=8,'fsdp'=2] {'dp'}, dimensions={0}, use_global_device_ids=true | all-gather | bytes 2304 | tf_op jit(solution)/shard_map/all_gather | solution.py:304
  1017.2 18.2 %all-gather = bf16[8,32,2]{1,2,0:T(2,128)(2,1)S(1)} all-gather(bf16[1,32,2]{1,2,0:T(2,128)(2,1)S(1)} %bitcast.609), channel_id=1, replica_groups=mesh['section'=2,'dp'=8,'fsdp'=2] {'dp'}, dimensions={0}, use_global_device_ids=true | all-gather | bytes 1152 | tf_op jit(solution)/shard_map/all_gather | solution.py:298
  1037.6 13.7 %reduce-scatter.21.cloned.1.call-done = f32[32,6]{1,0:T(8,128)} async-done(((f32[512,6]{1,0:T(8,128)}), f32[32,6]{1,0:T(8,128)}) %reduce-scatter.21.cloned.1.call-update) | async-done | bytes 784
  1052.1 26.0 %all-gather.1 = bf16[8,32,6]{1,2,0:T(8,128)(2,1)S(1)} all-gather(bf16[1,32,6]{1,2,0:T(8,128)(2,1)S(1)} %bitcast.604), channel_id=1, replica_groups=mesh['section'=2,'dp'=8,'fsdp'=2] {'dp'}, dimensions={0}, use_global_device_ids=true | all-gather | bytes 3456 | tf_op jit(solution)/shard_map/all_gather | solution.py:301
  1079.3 48.5 %reduce-scatter.13.cloned.1.call-done = f32[32,512]{1,0:T(8,128)} async-done(((f32[512,512]{1,0:T(8,128)}), f32[32,512]{1,0:T(8,128)}) %reduce-scatter.13.cloned.1.call-update) | async-done | bytes 65552 | tf_op jit(solution)/shard_map/reduce_scatter | solution.py:285
  1128.7 31.0 %all_gather.50 = bf16[256,512]{1,0:T(8,128)(2,1)S(1)} all-gather(bf16[32,512]{1,0:T(8,128)(2,1)S(1)} %convert_element_type.731), channel_id=1, replica_groups=mesh['section'=2,'dp'=8,'fsdp'=2] {'dp'}, dimensions={0}, use_global_device_ids=true | all-gather | bytes 294912 | tf_op jit(solution)/shard_map/all_gather | solution.py:295
  1160.5 99.8 %reduce-scatter.11.cloned.1.call-done = f32[32,1536]{1,0:T(8,128)} async-done(((f32[512,1536]{1,0:T(8,128)}), f32[32,1536]{1,0:T(8,128)}) %reduce-scatter.11.cloned.1.call-update) | async-done | bytes 196624 | tf_op jit(solution)/shard_map/reduce_scatter | solution.py:284
  1261.3 32.8 %all_gather.49 = bf16[256,1536]{1,0:T(8,128)(2,1)S(1)} all-gather(bf16[32,1536]{1,0:T(8,128)(2,1)S(1)} %convert_element_type.730), channel_id=1, replica_groups=mesh['section'=2,'dp'=8,'fsdp'=2] {'dp'}, dimensions={0}, use_global_device_ids=true | all-gather | bytes 884736 | tf_op jit(solution)/shard_map/all_gather | solution.py:294
  1295.4 8.5 all-gather.17.cloned.1.call-done
  1306.7 39.6 %all-gather.15.cloned.1.call-done = bf16[256,2048]{1,0:T(8,128)(2,1)} async-done(((bf16[32,2048]{1,0:T(8,128)(2,1)}), bf16[256,2048]{1,0:T(8,128)(2,1)}) %all-gather.15.cloned.1.call-update) | async-done | bytes 1048592 | tf_op jit(solution)/shard_map/all_gather | solution.py:296
  (976 shorter events, 782.2 us)
Async XLA Ops:
  7.2 38.0 %all-gather.9.cloned.1.call-start = ((), (), s32[]{:S(2)}) async-start(), calls=%async_computation.6 | async-start | bytes 2359296 | tf_op jit(solution)/shard_map/all_gather | solution.py:213
  8.0 71.9 %all-gather.11.cloned.1.call-start = ((), (), s32[]{:S(2)}) async-start(), calls=%async_computation.7 | async-start | bytes 3145728 | tf_op jit(solution)/shard_map/all_gather | solution.py:215
  8.8 105.9 %all-gather.13.cloned.1.call-start = ((), (), s32[]{:S(2)}) async-start(), calls=%async_computation.8 | async-start | bytes 3145728 | tf_op jit(solution)/shard_map/all_gather | solution.py:216
  9.5 903.6 %reduce-scatter.17.cloned.1.call-start = ((), (), s32[]{:S(2)}) async-start(), calls=%async_computation.13 | async-start | bytes 4456448 | tf_op jit(solution)/shard_map/reduce_scatter | solution.py:287
  14.7 64.2 %copy-start.115 = (f32[1,1,512]{2,1,0:T(1,128)}, f32[1,1,512]{2,1,0:T(1,128)S(1)}, u32[]{:S(2)}) copy-start(f32[1,1,512]{2,1,0:T(1,128)S(1)} %get-tuple-element.576) | copy-start | bytes 6148
  14.7 128.2 %copy-start.111 = (f32[1,1,512]{2,1,0:T(1,128)}, f32[1,1,512]{2,1,0:T(1,128)S(1)}, u32[]{:S(2)}) copy-start(f32[1,1,512]{2,1,0:T(1,128)S(1)} %get-tuple-element.577) | copy-start | bytes 6148
  19.2 95.5 %copy-start.189 = (f32[1,1,512]{2,1,0:T(1,128)}, f32[1,1,512]{2,1,0:T(1,128)S(1)}, u32[]{:S(2)}) copy-start(f32[1,1,512]{2,1,0:T(1,128)S(1)} %get-tuple-element.561) | copy-start | bytes 6148
  19.2 123.7 %copy-start.147 = (f32[1,1,512]{2,1,0:T(1,128)}, f32[1,1,512]{2,1,0:T(1,128)S(1)}, u32[]{:S(2)}) copy-start(f32[1,1,512]{2,1,0:T(1,128)S(1)} %get-tuple-element.566) | copy-start | bytes 6148
  23.5 91.1 %copy-start.124 = (f32[1,2048]{1,0:T(1,128)}, f32[1,2048]{1,0:T(1,128)S(1)}, u32[]{:S(2)}) copy-start(f32[1,2048]{1,0:T(1,128)S(1)} %add.865) | copy-start | bytes 24580
  40.6 386.4 %copy-start.9 = (bf16[1,512,512]{2,1,0:T(8,128)(2,1)}, bf16[1,512,512]{2,1,0:T(8,128)(2,1)S(1)}, u32[]{:S(2)}) copy-start(bf16[1,512,512]{2,1,0:T(8,128)(2,1)S(1)} %all_gather.45) | copy-start | bytes 1572868
  42.8 102.3 %copy-start.175 = (f32[1536]{0:T(1024)}, f32[1536]{0:T(1024)S(1)}, u32[]{:S(2)}) copy-start(f32[1536]{0:T(1024)S(1)} %pad_maximum_fusion.27) | copy-start | bytes 18436
  133.8 3.6 collective-permute-start
  190.4 13.1 collective-permute-start.1
  211.0 240.8 %copy-start.4 = (f32[1,3,196,512]{3,2,1,0:T(8,128)}, f32[1,3,196,512]{3,2,1,0:T(8,128)S(1)}, u32[]{:S(2)}) copy-start(f32[1,3,196,512]{3,2,1,0:T(8,128)S(1)} %get-tuple-element.527) | copy-start | bytes 3612676
  211.0 249.9 %copy-start.2 = (f32[1,3,196,512]{3,2,1,0:T(8,128)}, f32[1,3,196,512]{3,2,1,0:T(8,128)S(1)}, u32[]{:S(2)}) copy-start(f32[1,3,196,512]{3,2,1,0:T(8,128)S(1)} %get-tuple-element.525) | copy-start | bytes 3612676
  580.0 20.3 %collective-permute-start.2 = (bf16[3,196,512]{2,1,0:T(8,128)(2,1)S(1)}, bf16[3,196,512]{2,1,0:T(8,128)(2,1)S(1)}, u32[]{:S(2)}, u32[]{:S(2)}) collective-permute-start(bf16[3,196,512]{2,1,0:T(8,128)(2,1)S(1)} %convert_element_type.671), channel_id=1, source_target_pairs={{16,0},{17,1},{18,2},{19,3},{20,4},{21,5},{22,6},{23,7},{24,8},{25... | collective-permute-start | bytes 1806344 | tf_op jit(solution)/shard_map/ppermute | solution.py:25
  672.4 14.8 %collective-permute-start.3 = (bf16[3,196,512]{2,1,0:T(8,128)(2,1)S(1)}, bf16[3,196,512]{2,1,0:T(8,128)(2,1)S(1)}, u32[]{:S(2)}, u32[]{:S(2)}) collective-permute-start(bf16[3,196,512]{2,1,0:T(8,128)(2,1)S(1)} %convert_element_type.699), channel_id=1, source_target_pairs={{16,0},{17,1},{18,2},{19,3},{20,4},{21,5},{22,6},{23,7},{24,8},{25... | collective-permute-start | bytes 1806344 | tf_op jit(solution)/shard_map/ppermute | solution.py:25
  699.0 317.3 %reduce-scatter.19.cloned.1.call-start = ((), (), s32[]{:S(2)}) async-start(), calls=%async_computation.15 | async-start | bytes 278528
  777.8 257.5 %reduce-scatter.15.cloned.1.call-start = ((), (), s32[]{:S(2)}) async-start(), calls=%async_computation.11 | async-start | bytes 4456448 | tf_op jit(solution)/shard_map/reduce_scatter | solution.py:286
  786.9 264.3 %reduce-scatter.21.cloned.1.call-start = ((), (), s32[]{:S(2)}) async-start(), calls=%async_computation.16 | async-start | bytes 278528
  845.0 282.9 %reduce-scatter.13.cloned.1.call-start = ((), (), s32[]{:S(2)}) async-start(), calls=%async_computation.10 | async-start | bytes 1114112 | tf_op jit(solution)/shard_map/reduce_scatter | solution.py:285
  848.6 411.7 %reduce-scatter.11.cloned.1.call-start = ((), (), s32[]{:S(2)}) async-start(), calls=%async_computation.9 | async-start | bytes 3342336 | tf_op jit(solution)/shard_map/reduce_scatter | solution.py:284
  859.1 444.8 %all-gather.17.cloned.1.call-start = ((), (), s32[]{:S(2)}) async-start(), calls=%async_computation.14 | async-start | bytes 1179648 | tf_op jit(solution)/shard_map/all_gather | solution.py:297
  914.8 431.4 %all-gather.15.cloned.1.call-start = ((), (), s32[]{:S(2)}) async-start(), calls=%async_computation.12 | async-start | bytes 1179648 | tf_op jit(solution)/shard_map/all_gather | solution.py:296
  (200 other events, 1198.4 us)
Sparse Core Ops, SparseCore 0:
  9.6 35.5 all-gather.8
  46.8 33.1 all-gather.10
  81.5 33.1 all-gather.12
  699.1 103.2 reduce-scatter.16
  804.5 74.0 reduce-scatter.18
  880.9 93.7 reduce-scatter.14
  977.0 74.2 reduce-scatter.20
  1053.5 74.2 reduce-scatter.12
  1133.6 126.7 reduce-scatter.10
  1262.6 41.2 all-gather.16
  1306.8 39.4 all-gather.14
where the time goes:
time: 1370 us; the launch traced here: 1360 us
  local copies, waits for them, and re-layouts  403 us (29%)
  matrix products  315 us (23%)
  waiting for transfers between devices  263 us (19%)
  blocking collectives  228 us (17%)
  other arithmetic  119 us (9%)
  between operations  18.2 us (1%)
    reduce_scatter x1, waiting for transfers between devices, body(): lax.psum_scatter(s_qkv, ('dp', 'fsdp'), scatter_dimension=0, tiled=True)  99.8 us
    unnamed x1, blocking collectives  76.1 us
    reduce_scatter x1, waiting for transfers between devices, body(): lax.psum_scatter(s_proj, ('dp', 'fsdp'), scatter_dimension=0, tiled=True)  48.5 us
    dot_general x3, matrix products, layer_forward(): jnp.dot(active, fc2_w, preferred_element_type=jnp.float32) + bias_vals[5]  46.5 us
    all_gather x1, waiting for transfers between devices, body(): lax.all_gather(p_fc1.astype(jnp.bfloat16), 'dp', axis=0, tiled=True)  39.6 us
    dot_general x3, matrix products, layer_forward(): jnp.dot(normed_two, fc1_w, preferred_element_type=jnp.float32) + hidden_vals  36.9 us
    reshape x9, local copies, waits for them, and re-layouts, layer_forward(): values = packed[:, 2 * D:].reshape(head_shape)  36.8 us
    all_gather x1, waiting for transfers between devices, body(): lax.all_gather(fc2_w, 'fsdp', axis=1, tiled=True)  34.7 us
  transfers between devices with their start and end apart: 15, of which 11 were waited for; matrix products, arithmetic and copies ran while one was open for 22% of the time, Pallas kernels for 0%

commit v1 on v0

v1 whole, which is shorter than its diff:
```python
import functools

import jax
import jax.numpy as jnp
import numpy as np
from jax import lax
from jax.experimental import pallas as pl
from jax.experimental.pallas import tpu as pltpu
from jax.sharding import PartitionSpec as P

D = 512
FF = 2048
HEADS = 16
HEAD_DIM = 32
GRID = 14
WIN = 7
TOK = 196
WTOK = 49
NWIN = 4
TABLE = 169
MB = 2
PAIR = 112
ROWS = 2 * PAIR
LANES = 128
GROUP = LANES // HEAD_DIM

EPS = 1e-05
SCALE = HEAD_DIM ** (-0.5)
NEG = -1e30
HIGH = lax.Precision.HIGHEST
F32 = jnp.float32
BF16 = jnp.bfloat16


def order_matrix(layer):
    moved = (WIN // 2) if layer else 0
    place = np.zeros((ROWS, TOK), np.float32)
    for wi in range(2):
        for wj in range(2):
            for ti in range(WIN):
                for tj in range(WIN):
                    row = wi * PAIR + wj * WTOK + ti * WIN + tj
                    i = (wi * WIN + ti + moved) % GRID
                    j = (wj * WIN + tj + moved) % GRID
                    place[row, i * GRID + j] = 1.0
    return place


def dot(a, b):
    return lax.dot_general(a, b, (((1,), (0,)), ((), ())), preferred_element_type=F32)


def dot_nt(a, b):
    return lax.dot_general(a, b, (((1,), (1,)), ((), ())), preferred_element_type=F32)


def dot_tn(a, b):
    return lax.dot_general(a, b, (((0,), (0,)), ((), ())), preferred_element_type=F32)


def normalised(values):
    centred = values - jnp.mean(values, -1, keepdims=True)
    inverse = lax.rsqrt(jnp.mean(centred * centred, -1, keepdims=True) + EPS)
    return centred * inverse, inverse


def norm_back(upstream, gain, unit, inverse):
    d_unit = upstream * gain
    return inverse * (
        d_unit
        - jnp.mean(d_unit, -1, keepdims=True)
        - unit * jnp.mean(d_unit * unit, -1, keepdims=True)
    )


def head_masks():
    lane = lax.broadcasted_iota(jnp.int32, (PAIR, LANES), 1)
    return [
        jnp.where((lane >= j * HEAD_DIM) & (lane < (j + 1) * HEAD_DIM), 1.0, 0.0).astype(BF16)
        for j in range(GROUP)
    ]


def softmax(query, keys, bias):
    scores = dot_nt(query, keys) * SCALE + bias
    raised = jnp.exp(scores - jnp.max(scores, -1, keepdims=True))
    return raised / jnp.sum(raised, -1, keepdims=True)


def forward_kernel(
    place, place_t, x, qkv_w, proj_w, fc1_w, fc2_w, vec, hidden_bias, bias,
    y, windows, packed, mixed, middle, normed2, slope, active,
):
    source = dot(place[...], x[0])
    unit, _ = normalised(source)
    windows[0] = (unit * vec[0:1] + vec[2:3]).astype(BF16)
    win = windows[0]
    packed[0, :, :D] = (dot(win, qkv_w[:, :D]) + vec[3:4]).astype(BF16)
    packed[0, :, D : 2 * D] = dot(win, qkv_w[:, D : 2 * D]).astype(BF16)
    packed[0, :, 2 * D :] = (dot(win, qkv_w[:, 2 * D :]) + vec[4:5]).astype(BF16)
    masks = head_masks()
    for pair in range(2):
        rows = slice(pair * PAIR, (pair + 1) * PAIR)
        for group in range(HEADS // GROUP):
            at = group * LANES
            query = packed[0, rows, at : at + LANES]
            keys = packed[0, rows, D + at : D + at + LANES]
            values = packed[0, rows, 2 * D + at : 2 * D + at + LANES]
            total = None
            for j in range(GROUP):
                probs = softmax(query * masks[j], keys, bias[pair, group * GROUP + j])
                part = dot(probs.astype(BF16), values * masks[j])
                total = part if total is None else total + part
            mixed[0, rows, at : at + LANES] = total.astype(BF16)
    mid = source + dot(mixed[0], proj_w[...]) + vec[5:6]
    middle[0] = mid
    unit2, _ = normalised(mid)
    normed2[0] = (unit2 * vec[1:2] + vec[6:7]).astype(BF16)
    low = normed2[0]
    for c in range(FF // D):
        cols = slice(c * D, (c + 1) * D)
        hidden = dot(low, fc1_w[:, cols]) + hidden_bias[0:1, cols]
        half = 0.5 * (1.0 + lax.erf(hidden * 0.7071067811865476))
        active[0, :, cols] = (hidden * half).astype(BF16)
        bell = jnp.exp(-0.5 * hidden * hidden) * 0.3989422804014327
        slope[0, :, cols] = (half + hidden * bell).astype(BF16)
    out = mid + (dot(active[0], fc2_w[...]) + vec[7:8])
    y[0] = dot(place_t[...], out.astype(BF16)).astype(BF16)


def backward_kernel(
    place, place_t, x, up, qkv_w, proj_w, fc1_w, fc2_w, vec, bias, packed, middle, slope,
    d_x, up_rows, d_hidden, d_projected, d_packed, d_vec, d_hidden_bias, d_rel,
):
    @pl.when(pl.program_id(0) == 0)
    def _():
        d_vec[...] = jnp.zeros_like(d_vec)
        d_hidden_bias[...] = jnp.zeros_like(d_hidden_bias)
        d_rel[...] = jnp.zeros_like(d_rel)

    def add_row(row, values):
        d_vec[row : row + 1] += jnp.sum(values, 0, keepdims=True)

    upstream = dot(place[...], up[0])
    up_low = upstream.astype(BF16)
    up_rows[0] = up_low
    add_row(7, upstream)
    for c in range(FF // D):
        cols = slice(c * D, (c + 1) * D)
        d_active = dot_nt(up_low, fc2_w[cols])
        d_hid = (slope[0, :, cols].astype(F32) * d_active).astype(BF16)
        d_hidden[0, :, cols] = d_hid
        d_hidden_bias[0:1, cols] += jnp.sum(d_hid.astype(F32), 0, keepdims=True)
    d_normed2 = dot_nt(d_hidden[0], fc1_w[...])
    unit2, inverse2 = normalised(middle[0])
    add_row(1, d_normed2 * unit2)
    add_row(6, d_normed2)
    d_middle = upstream + norm_back(d_normed2, vec[1:2], unit2, inverse2)
    d_proj = d_middle.astype(BF16)
    d_projected[0] = d_proj
    add_row(5, d_proj.astype(F32))
    d_mixed = dot_nt(d_proj, proj_w[...]).astype(BF16)
    masks = head_masks()
    for pair in range(2):
        rows = slice(pair * PAIR, (pair + 1) * PAIR)
        for group in range(HEADS // GROUP):
            at = group * LANES
            query = packed[0, rows, at : at + LANES]
            keys = packed[0, rows, D + at : D + at + LANES]
            values = packed[0, rows, 2 * D + at : 2 * D + at + LANES]
            d_mix = d_mixed[rows, at : at + LANES]
            d_query = d_keys = d_values = None
            for j in range(GROUP):
                head = group * GROUP + j
                query_j = query * masks[j]
                d_mix_j = d_mix * masks[j]
                probs = softmax(query_j, keys, bias[pair, head])
                d_probs = dot_nt(d_mix_j, values)
                d_scores = probs * (d_probs - jnp.sum(probs * d_probs, -1, keepdims=True))
                d_low = d_scores.astype(BF16)
                d_rel[head] += d_low.astype(F32)
                one = dot(d_low, keys * masks[j])
                two = dot_tn(d_low, query_j)
                three = dot_tn(probs.astype(BF16), d_mix_j)
                d_query = one if j == 0 else d_query + one
                d_keys = two if j == 0 else d_keys + two
                d_values = three if j == 0 else d_values + three
            d_packed[0, rows, at : at + LANES] = (d_query * SCALE).astype(BF16)
            d_packed[0, rows, D + at : D + at + LANES] = (d_keys * SCALE).astype(BF16)
            d_packed[0, rows, 2 * D + at : 2 * D + at + LANES] = d_values.astype(BF16)
    add_row(3, d_packed[0, :, :D].astype(F32))
    add_row(4, d_packed[0, :, 2 * D :].astype(F32))
    d_windows = dot_nt(d_packed[0], qkv_w[...])
    unit, inverse = normalised(dot(place[...], x[0]))
    add_row(0, d_windows * unit)
    add_row(2, d_windows)
    d_source = d_middle + norm_back(d_windows, vec[0:1], unit, inverse)
    d_x[0] = dot(place_t[...], d_source.astype(BF16)).astype(BF16)


def whole(shape):
    return pl.BlockSpec(shape, lambda i: (0,) * len(shape))


def each(rows, cols):
    return pl.BlockSpec((1, rows, cols), lambda i: (i, 0, 0))


PARAMS = pltpu.CompilerParams(
    dimension_semantics=("arbitrary",), vmem_limit_bytes=58 * 1024 * 1024
)
WEIGHT_SPECS = [whole((D, 3 * D)), whole((D, D)), whole((D, FF)), whole((FF, D))]
BIAS_SHAPE = (2, HEADS, PAIR, PAIR)


def layer_forward(x, order, weights, vec, hidden_bias, bias):
    count = x.shape[0]
    saved = [(D, BF16), (3 * D, BF16), (D, BF16), (D, F32), (D, BF16), (FF, BF16), (FF, BF16)]
    return pl.pallas_call(
        forward_kernel,
        grid=(count,),
        in_specs=[whole((ROWS, TOK)), whole((TOK, ROWS)), each(TOK, D)]
        + WEIGHT_SPECS
        + [whole((8, D)), whole((1, FF)), whole(BIAS_SHAPE)],
        out_specs=[each(TOK, D)] + [each(ROWS, width) for width, _ in saved],
        out_shape=[jax.ShapeDtypeStruct((count, TOK, D), BF16)]
        + [jax.ShapeDtypeStruct((count, ROWS, width), kind) for width, kind in saved],
        compiler_params=PARAMS,
        cost_estimate=pl.CostEstimate(
            flops=count * 2_000_000_000, bytes_accessed=20_000_000, transcendentals=0
        ),
        name="layer_forward",
    )(*order, x, *weights, vec, hidden_bias, bias)


def layer_backward(x, up, order, weights, vec, bias, packed, middle, slope):
    count = x.shape[0]
    rows = [(D, BF16), (FF, BF16), (D, BF16), (3 * D, BF16)]
    sums = [(8, D), (8, FF), (HEADS, PAIR, PAIR)]
    return pl.pallas_call(
        backward_kernel,
        grid=(count,),
        in_specs=[whole((ROWS, TOK)), whole((TOK, ROWS)), each(TOK, D), each(TOK, D)]
        + WEIGHT_SPECS
        + [whole((8, D)), whole(BIAS_SHAPE), each(ROWS, 3 * D), each(ROWS, D), each(ROWS, FF)],
        out_specs=[each(TOK, D)]
        + [each(ROWS, width) for width, _ in rows]
        + [whole(shape) for shape in sums],
        out_shape=[jax.ShapeDtypeStruct((count, TOK, D), BF16)]
        + [jax.ShapeDtypeStruct((count, ROWS, width), kind) for width, kind in rows]
        + [jax.ShapeDtypeStruct(shape, F32) for shape in sums],
        compiler_params=PARAMS,
        cost_estimate=pl.CostEstimate(
            flops=count * 5_000_000_000, bytes_accessed=30_000_000, transcendentals=0
        ),
        name="layer_backward",
    )(*order, x, up, *weights, vec, bias, packed, middle, slope)


def swap(block):
    return lax.ppermute(block, "section", [(0, 1), (1, 0)])


def both_layers(piece):
    return lax.all_gather(piece, "section", axis=0, tiled=True)


def bias_blocks(onehot, table, differs):
    rel = jnp.dot(onehot, table, precision=HIGH).T.reshape(1, HEADS, WTOK, WTOK)
    if differs is None:
        blocks = jnp.broadcast_to(rel, (NWIN, HEADS, WTOK, WTOK))
    else:
        blocks = rel + jnp.where(differs, -100.0, 0.0)[:, None]
    blocks = blocks.reshape(2, 2, HEADS, WTOK, WTOK)
    last = PAIR - 2 * WTOK
    first = jnp.pad(
        blocks[:, 0], ((0, 0), (0, 0), (0, 0), (0, WTOK + last)), constant_values=NEG
    )
    second = jnp.pad(blocks[:, 1], ((0, 0), (0, 0), (0, 0), (WTOK, last)), constant_values=NEG)
    joined = jnp.concatenate([first, second], 2)
    return jnp.pad(joined, ((0, 0), (0, 0), (0, last), (0, 0)), constant_values=NEG)


def weight_sums(saved, grads, wide):
    windows, mixed, normed2, active = (v.reshape(-1, v.shape[-1]) for v in saved)
    up_rows, d_hidden, d_projected, d_packed = (v.reshape(-1, v.shape[-1]) for v in grads)
    g_fc2 = dot_tn(active, up_rows).astype(BF16)
    g_fc1 = dot_tn(normed2, d_hidden).astype(BF16)
    g_proj = dot_tn(mixed, d_projected).astype(BF16)
    g_qkv = dot_tn(windows, d_packed).astype(BF16)
    blocks = [g_fc2.reshape(wide, -1, D), g_proj.reshape(wide, -1, D)]
    blocks += [g_qkv[:, c * D : (c + 1) * D].reshape(wide, -1, D) for c in range(3)]
    blocks += [g_fc1[:, c * D : (c + 1) * D].reshape(wide, -1, D) for c in range(FF // D)]
    joined = jnp.concatenate(blocks, 1).reshape(-1, D)
    return lax.psum_scatter(
        joined, ("fsdp", "dp", "section"), scatter_dimension=0, tiled=True
    )


def body(
    images, out_grad, live, qkv_w, proj_w, fc1_w, fc2_w, gains, biases, hidden_bias, table,
    rel_index, region,
):
    section = lax.axis_index("section")
    wide = lax.axis_size("fsdp")
    count = images.shape[0] // MB
    mine = lax.dynamic_slice_in_dim(images, section * count, count, 0)
    cotangent = lax.dynamic_slice_in_dim(out_grad, section * count, count, 0)
    limit = lax.dynamic_slice_in_dim(live[0], section, 1, 0)
    keep = jnp.arange(count, dtype=jnp.int32) < limit
    cotangent = jnp.where(keep[:, None, None], cotangent, jnp.zeros((), BF16))

    gathered = [
        both_layers(lax.all_gather(w, "fsdp", axis=1, tiled=True))
        for w in (qkv_w, proj_w, fc1_w, fc2_w)
    ]
    joined = jnp.concatenate([gains, biases, hidden_bias.reshape(1, -1, gains.shape[-1])], 1)
    joined = both_layers(lax.all_gather(joined, "fsdp", axis=0, tiled=False))
    joined = joined.reshape(2, wide, -1, gains.shape[-1]).astype(F32)
    tables = both_layers(table)
    onehot = (rel_index.reshape(-1)[:, None] == jnp.arange(TABLE, dtype=jnp.int32)[None, :]).astype(
        F32
    )
    region_win = region.reshape(2, WIN, 2, WIN).transpose(0, 2, 1, 3).reshape(NWIN, WTOK)
    differs = region_win[:, :, None] != region_win[:, None, :]

    layers = []
    for layer in range(2):
        vec = joined[layer, :, :8].transpose(1, 0, 2).reshape(8, D)
        hidden = joined[layer, :, 8:].reshape(1, FF)
        bias = bias_blocks(onehot, tables[layer], differs if layer else None)
        place = order_matrix(layer)
        order = (jnp.asarray(place, BF16), jnp.asarray(place.T, BF16))
        layers.append((order, tuple(w[layer] for w in gathered), vec, hidden, bias))

    kept = []
    x = mine
    for order, weights, vec, hidden, bias in layers:
        y, *saved = layer_forward(x, order, weights, vec, hidden, bias)
        kept.append((x, saved))
        x = y
    outs = (kept[1][0], x)

    up = cotangent
    input_grads, pieces, smalls = [None, None], [None, None], [None, None]
    for layer in (1, 0):
        order, weights, vec, _, bias = layers[layer]
        source, (windows, packed, mixed, middle, normed2, slope, active) = kept[layer]
        up, *rows, d_vec, d_hidden_bias, d_rel = layer_backward(
            source, up, order, weights, vec, bias, packed, middle, slope
        )
        input_grads[layer] = up
        pieces[layer] = weight_sums((windows, mixed, normed2, active), rows, wide)
        d_rel = d_rel[:, :WTOK, :WTOK] + d_rel[:, WTOK : 2 * WTOK, WTOK : 2 * WTOK]
        d_table = jnp.einsum("pt,hp->th", onehot, d_rel.reshape(HEADS, -1), precision=HIGH)
        smalls[layer] = jnp.concatenate(
            [d_vec.reshape(-1), d_hidden_bias[0], d_table.reshape(-1)]
        )

    total = lax.psum(jnp.stack(smalls), ("section", "dp", "fsdp"))
    total = lax.dynamic_index_in_dim(total, section, 0, keepdims=False)
    part = lax.axis_index("fsdp")
    d_vec = total[: 8 * D].reshape(8, D)
    d_vec = lax.dynamic_slice_in_dim(d_vec, part * (D // wide), D // wide, 1)
    d_hidden_bias = lax.dynamic_slice_in_dim(
        total[8 * D : 8 * D + FF], part * (FF // wide), FF // wide, 0
    )
    d_table = total[8 * D + FF :].reshape(TABLE, HEADS)

    first_half = section == 0

    def exchange(first, second):
        own = jnp.where(first_half, first, second)
        other = swap(jnp.where(first_half, second, first))
        return jnp.concatenate(
            [jnp.where(first_half, own, other), jnp.where(first_half, other, own)], 0
        )

    layer_out = exchange(*outs)
    input_grad = exchange(*input_grads)
    own = exchange(*pieces)
    rows = lax.all_gather(own, "dp", axis=0, tiled=True).astype(F32)
    deep, thin = FF // wide, D // wide
    o_fc2, rows = rows[:deep], rows[deep:]
    o_proj, rows = rows[:thin], rows[thin:]
    o_qkv = jnp.concatenate([rows[c * thin : (c + 1) * thin] for c in range(3)], 1)
    rows = rows[3 * thin :]
    o_fc1 = jnp.concatenate([rows[c * thin : (c + 1) * thin] for c in range(FF // D)], 1)
    return (
        layer_out[None],
        input_grad[None],
        o_qkv[None],
        o_proj[None],
        o_fc1[None],
        o_fc2[None],
        d_vec[:2][None],
        d_vec[2:][None],
        d_hidden_bias[None],
        d_table[None],
        d_vec[3][None],
    )


def solution(mesh):
    return jax.shard_map(
        body,
        mesh=mesh,
        in_specs=(
            P(("dp", "fsdp"), None, None),
            P(("dp", "fsdp"), None, None),
            P(("dp", "fsdp"), None),
            P("section", "fsdp", None),
            P("section", "fsdp", None),
            P("section", "fsdp", None),
            P("section", "fsdp", None),
            P("section", None, "fsdp"),
            P("section", None, "fsdp"),
            P("section", "fsdp"),
            P("section", None, None),
            P(),
            P(),
        ),
        out_specs=(
            P("section", ("dp", "fsdp"), None, None),
            P("section", ("dp", "fsdp"), None, None),
            P("section", "fsdp", None),
            P("section", "fsdp", None),
            P("section", "fsdp", None),
            P("section", "fsdp", None),
            P("section", None, "fsdp"),
            P("section", None, "fsdp"),
            P("section", "fsdp"),
            P("section", None, None),
            P("section", "fsdp"),
        ),
        check_vma=False,
    )
```

time: 1370 us -> 777 us (0.57)
  local copies, waits for them, and re-layouts: 403 us -> 56 us
  matrix products: 315 us -> 20.6 us
  waiting for transfers between devices: 263 us -> 502 us
  blocking collectives: 228 us -> 18 us
  Pallas kernels: 0 us -> 136 us
  other arithmetic: 119 us -> 17.4 us
    dot_general x79 -> x12, matrix products: 293 us -> 20.6 us  [the longest x8 14.3 us: dot_tn(): lax.dot_general(a, b, (((0,), (0,)), ((), ())), preferred_element_type=F32)]
    reshape x93 -> x7, local copies, waits for them, and re-layouts: 214 us -> 0.63 us  [the longest x2 0.33 us: body(): d_rel.reshape(HEADS, -1)]
    pallas_call x0 -> x4, Pallas kernels: none -> 136 us  [the longest x2 96.3 us: layer_backward(): pl.pallas_call(backward_kernel, grid=(count,), in_specs=[whole((ROWS, TOK...]
    all_gather x9 -> x4, blocking collectives: 152 us -> 18 us  [the longest x1 10 us: body(): lax.all_gather(w, 'fsdp', axis=1, tiled=True)]
    psum x0 -> x1, waiting for transfers between devices: none -> 117 us  [body(): total = lax.psum(jnp.stack(smalls), ('section', 'dp', 'fsdp'))]
    all_gather x5 -> x8, waiting for transfers between devices: 85.8 us -> 172 us  [the longest x3 89.2 us: body(): lax.all_gather(w, 'fsdp', axis=1, tiled=True)]
    unnamed x1 -> x0, blocking collectives: 76.1 us -> none
    reduce_sum x44 -> x0, other arithmetic: 71.6 us -> none  [the longest x12 23 us: norm(): middle = jnp.mean(values, -1, keepdims=True)]
  transfers between devices with their start and end apart: 15 -> 14, of which waited for: 11 -> 11; matrix products, arithmetic and copies ran while one was open for 22% -> 8% of each run, Pallas kernels for 0% -> 0%
where the time goes in v1:
time: 777 us; the launch traced here: 766 us
  waiting for transfers between devices  502 us (65%)
  Pallas kernels  136 us (18%)
  local copies, waits for them, and re-layouts  56 us (7%)
  matrix products  20.6 us (3%)
  blocking collectives  18 us (2%)
  other arithmetic  17.4 us (2%)
  between operations  14.8 us (2%)
    reduce_scatter x2, waiting for transfers between devices, weight_sums(): lax.psum_scatter(joined, ('fsdp', 'dp', 'section'), scatter_dimension=0,...  210 us
    psum x1, waiting for transfers between devices, body(): total = lax.psum(jnp.stack(smalls), ('section', 'dp', 'fsdp'))  117 us
    pallas_call x2, Pallas kernels, layer_backward(): pl.pallas_call(backward_kernel, grid=(count,), in_specs=[whole((ROWS, TOK...  96.3 us
    all_gather x3, waiting for transfers between devices, body(): lax.all_gather(w, 'fsdp', axis=1, tiled=True)  89.2 us
    all_gather x1, waiting for transfers between devices, body(): rows = lax.all_gather(own, 'dp', axis=0, tiled=True).astype(F32)  55.9 us
    pallas_call x2, Pallas kernels, layer_forward(): pl.pallas_call(forward_kernel, grid=(count,), in_specs=[whole((ROWS, TOK)...  39.4 us
    all_gather x4, waiting for transfers between devices, both_layers(): return lax.all_gather(piece, 'section', axis=0, tiled=True)  27.4 us
    unnamed x87, local copies, waits for them, and re-layouts  22.3 us
  transfers between devices with their start and end apart: 14, of which 11 were waited for; matrix products, arithmetic and copies ran while one was open for 8% of the time, Pallas kernels for 0%

profile of v1, /device:TPU:0, one launch (start us, length us, event | category | flops | bytes accessed | tf_op | source)
XLA Modules:
  0.0 766.1 jit_solution(8614256696172163689)
XLA Ops:
  9.5 10.0 %all_gather.41 = bf16[1,512,512]{2,1,0:T(8,128)(2,1)} all-gather(bf16[1,256,512]{2,1,0:T(8,128)(2,1)S(1)} %copy-done.11), channel_id=1, replica_groups=mesh['section'=2,'dp'=8,'fsdp'=2] {'fsdp'}, dimensions={1}, use_global_device_ids=true | all-gather | bytes 786432 | tf_op jit(solution)/shard_map/all_gather | solution.py:314
  19.6 19.9 %all-gather.11.cloned.1.call-done = bf16[1,512,1536]{2,1,0:T(8,128)(2,1)} async-done(((bf16[1,256,1536]{2,1,0:T(8,128)(2,1)}), bf16[1,512,1536]{2,1,0:T(8,128)(2,1)}) %all-gather.11.cloned.1.call-update) | async-done | bytes 1572880 | tf_op jit(solution)/shard_map/all_gather | solution.py:314
  39.6 34.6 %all-gather.17.cloned.1.call-done = bf16[1,512,2048]{2,1,0:T(8,128)(2,1)} async-done(((bf16[1,256,2048]{2,1,0:T(8,128)(2,1)}), bf16[1,512,2048]{2,1,0:T(8,128)(2,1)}) %all-gather.17.cloned.1.call-update) | async-done | bytes 2097168 | tf_op jit(solution)/shard_map/all_gather | solution.py:314
  74.3 34.6 %all-gather.21.cloned.1.call-done = bf16[1,2048,512]{2,1,0:T(8,128)(2,1)} async-done(((bf16[1,1024,512]{2,1,0:T(8,128)(2,1)}), bf16[1,2048,512]{2,1,0:T(8,128)(2,1)}) %all-gather.21.cloned.1.call-update) | async-done | bytes 2097168 | tf_op jit(solution)/shard_map/all_gather | solution.py:314
  112.5 4.4 all-gather
  128.5 2.4 slice_bitcast_fusion.10
  130.9 3.3 all-gather.13.cloned.1.call-done
  134.1 3.7 slice_bitcast_fusion.5
  137.9 12.5 %all-gather.19.cloned.1.call-done = bf16[2,512,2048]{2,1,0:T(8,128)(2,1)} async-done(((bf16[1,512,2048]{2,1,0:T(8,128)(2,1)}), bf16[2,512,2048]{2,1,0:T(8,128)(2,1)}) %all-gather.19.cloned.1.call-update) | async-done | bytes 4194320 | tf_op jit(solution)/shard_map/all_gather | solution.py:265
  150.4 4.8 slice_bitcast_fusion.2
  155.2 11.6 %all-gather.23.cloned.1.call-done = bf16[2,2048,512]{2,1,0:T(8,128)(2,1)} async-done(((bf16[1,2048,512]{2,1,0:T(8,128)(2,1)}), bf16[2,2048,512]{2,1,0:T(8,128)(2,1)}) %all-gather.23.cloned.1.call-update) | async-done | bytes 4194320 | tf_op jit(solution)/shard_map/all_gather | solution.py:265
  166.8 4.5 slice_bitcast_fusion.1
  171.3 19.7 %layer_forward.2 = (bf16[3,196,512]{2,1,0:T(8,128)(2,1)}, bf16[3,224,512]{2,1,0:T(8,128)(2,1)}, bf16[3,224,1536]{2,1,0:T(8,128)(2,1)}, bf16[3,224,512]{2,1,0:T(8...) custom-call(bf16[224,196]{1,0:T(8,128)(2,1)} %constant.46.clone.plac, ...), custom_call_target="tpu_custom_call" | custom-call | flops 6000000000 | bytes 20000000 | tf_op jit(solution)/shard_map/layer_forward/pallas_call | solution.py:219
  191.0 19.7 %layer_forward.3 = (bf16[3,196,512]{2,1,0:T(8,128)(2,1)}, bf16[3,224,512]{2,1,0:T(8,128)(2,1)}, bf16[3,224,1536]{2,1,0:T(8,128)(2,1)}, bf16[3,224,512]{2,1,0:T(8...) custom-call(bf16[224,196]{1,0:T(8,128)(2,1)} %constant.48.clone.plac, ...), custom_call_target="tpu_custom_call" | custom-call | flops 6000000000 | bytes 20000000 | tf_op jit(solution)/shard_map/layer_forward/pallas_call | solution.py:219
  210.8 47.9 %layer_backward.2 = (bf16[3,196,512]{2,1,0:T(8,128)(2,1)}, bf16[3,224,512]{2,1,0:T(8,128)(2,1)}, bf16[3,224,2048]{2,1,0:T(8,128)(2,1)}, bf16[3,224,512]{2,1,0:T(...) custom-call(bf16[224,196]{1,0:T(8,128)(2,1)} %constant.48.clone.plac, ...), custom_call_target="tpu_custom_call" | custom-call | flops 15000000512 | bytes 30000000 | tf_op jit(solution)/shard_map/layer_backward/pallas_call | solution.py:240
  258.7 48.4 %layer_backward.3 = (bf16[3,196,512]{2,1,0:T(8,128)(2,1)}, bf16[3,224,512]{2,1,0:T(8,128)(2,1)}, bf16[3,224,2048]{2,1,0:T(8,128)(2,1)}, bf16[3,224,512]{2,1,0:T(...) custom-call(bf16[224,196]{1,0:T(8,128)(2,1)} %constant.46.clone.plac, ...), custom_call_target="tpu_custom_call" | custom-call | flops 15000000512 | bytes 30000000 | tf_op jit(solution)/shard_map/layer_backward/pallas_call | solution.py:240
  307.1 3.0 bitcast_convert_fusion.3
  327.4 3.6 bitcast_convert_fusion.1
  348.9 1.9 fusion.3
  351.8 90.1 %reduce-scatter.3.cloned.1.call-done = bf16[192,512]{1,0:T(8,128)(2,1)} async-done(((bf16[6144,512]{1,0:T(8,128)(2,1)}), bf16[192,512]{1,0:T(8,128)(2,1)}) %reduce-scatter.3.cloned.1.call-update) | async-done | bytes 196624 | tf_op jit(solution)/shard_map/reduce_scatter | solution.py:295
  442.0 120.1 %reduce-scatter.5.cloned.1.call-done = bf16[192,512]{1,0:T(8,128)(2,1)} async-done(((bf16[6144,512]{1,0:T(8,128)(2,1)}), bf16[192,512]{1,0:T(8,128)(2,1)}) %reduce-scatter.5.cloned.1.call-update) | async-done | bytes 196624 | tf_op jit(solution)/shard_map/reduce_scatter | solution.py:295
  568.7 116.8 %all-reduce.8.cloned.1.call-done = f32[2,8848]{1,0:T(2,128)} async-done(((f32[2,8848]{1,0:T(2,128)}), f32[2,8848]{1,0:T(2,128)}) %all-reduce.8.cloned.1.call-update) | async-done | bytes 70800 | tf_op jit(solution)/shard_map/psum | solution.py:360
  694.8 55.9 %all-gather.25.cloned.1.call-done = bf16[3072,512]{1,0:T(8,128)(2,1)} async-done(((bf16[384,512]{1,0:T(8,128)(2,1)}), bf16[3072,512]{1,0:T(8,128)(2,1)}) %all-gather.25.cloned.1.call-update) | async-done | bytes 3145744 | tf_op jit(solution)/shard_map/all_gather | solution.py:382
  750.6 2.8 convert_element_type.44
  (193 shorter events, 75.1 us)
Async XLA Ops:
  7.2 118.3 %copy-start = (s32[1,2]{1,0:T(1,128)S(1)}, s32[1,2]{1,0:T(1,128)}, u32[]{:S(2)}) copy-start(s32[1,2]{1,0:T(1,128)} %param.19) | copy-start | bytes 28
  7.2 32.3 %all-gather.11.cloned.1.call-start = ((), (), s32[]{:S(2)}) async-start(), calls=%async_computation.2 | async-start | bytes 2359296 | tf_op jit(solution)/shard_map/all_gather | solution.py:314
  7.9 66.3 %all-gather.17.cloned.1.call-start = ((), (), s32[]{:S(2)}) async-start(), calls=%async_computation.5 | async-start | bytes 3145728 | tf_op jit(solution)/shard_map/all_gather | solution.py:314
  8.7 100.2 %all-gather.21.cloned.1.call-start = ((), (), s32[]{:S(2)}) async-start(), calls=%async_computation.7 | async-start | bytes 3145728 | tf_op jit(solution)/shard_map/all_gather | solution.py:314
  9.4 119.1 %all-gather.15.cloned.1.call-start = ((), (), s32[]{:S(2)}) async-start(), calls=%async_computation.4 | async-start | bytes 1572864 | tf_op jit(solution)/shard_map/all_gather | solution.py:265
  19.5 114.6 %all-gather.13.cloned.1.call-start = ((), (), s32[]{:S(2)}) async-start(), calls=%async_computation.3 | async-start | bytes 4718592 | tf_op jit(solution)/shard_map/all_gather | solution.py:265
  39.6 110.9 %all-gather.19.cloned.1.call-start = ((), (), s32[]{:S(2)}) async-start(), calls=%async_computation.6 | async-start | bytes 6291456 | tf_op jit(solution)/shard_map/all_gather | solution.py:265
  74.2 34.8 %copy-start.12 = (s32[49,49]{1,0:T(8,128)S(1)}, s32[49,49]{1,0:T(8,128)}, u32[]{:S(2)}) copy-start(s32[49,49]{1,0:T(8,128)} %param.28) | copy-start | bytes 28816
  74.2 34.9 %copy-start.13 = (f32[1,169,16]{1,2,0:T(8,128)S(1)}, f32[1,169,16]{1,2,0:T(8,128)}, u32[]{:S(2)}) copy-start(f32[1,169,16]{1,2,0:T(8,128)} %param.27) | copy-start | bytes 32452
  74.3 38.2 %copy-start.16 = (bf16[1,1024]{1,0:T(2,128)(2,1)S(1)}, bf16[1,1024]{1,0:T(2,128)(2,1)}, u32[]{:S(2)}) copy-start(bf16[1,1024]{1,0:T(2,128)(2,1)} %param.26) | copy-start | bytes 6148
  74.3 38.2 %copy-start.17 = (bf16[1,6,256]{2,1,0:T(8,128)(2,1)S(1)}, bf16[1,6,256]{2,1,0:T(8,128)(2,1)}, u32[]{:S(2)}) copy-start(bf16[1,6,256]{2,1,0:T(8,128)(2,1)} %param.25) | copy-start | bytes 9220
  74.3 38.2 %copy-start.18 = (bf16[1,2,256]{2,1,0:T(2,128)(2,1)S(1)}, bf16[1,2,256]{2,1,0:T(2,128)(2,1)}, u32[]{:S(2)}) copy-start(bf16[1,2,256]{2,1,0:T(2,128)(2,1)} %param.24) | copy-start | bytes 3076
  74.3 92.5 %all-gather.23.cloned.1.call-start = ((), (), s32[]{:S(2)}) async-start(), calls=%async_computation.8 | async-start | bytes 6291456 | tf_op jit(solution)/shard_map/all_gather | solution.py:265
  108.9 11.9 %copy-start.19 = (s32[196]{0:T(256)S(1)}, s32[196]{0:T(256)}, u32[]{:S(2)}) copy-start(s32[196]{0:T(256)} %param.29) | copy-start | bytes 2356
  109.0 333.0 %reduce-scatter.3.cloned.1.call-start = ((), (), s32[]{:S(2)}) async-start(), calls=%async_computation.9 | async-start | bytes 6488064 | tf_op jit(solution)/shard_map/reduce_scatter | solution.py:295
  258.6 48.4 %copy-start.30 = (bf16[3,224,2048]{2,1,0:T(8,128)(2,1)S(1)}, bf16[3,224,2048]{2,1,0:T(8,128)(2,1)}, u32[]{:S(2)}) copy-start(bf16[3,224,2048]{2,1,0:T(8,128)(2,1)} %get-tuple-element.53) | copy-start | bytes 8257540
  326.4 235.7 %reduce-scatter.5.cloned.1.call-start = ((), (), s32[]{:S(2)}) async-start(), calls=%async_computation.10 | async-start | bytes 6488064 | tf_op jit(solution)/shard_map/reduce_scatter | solution.py:295
  344.1 341.4 %all-reduce.8.cloned.1.call-start = ((), (), s32[]{:S(2)}) async-start(), calls=%async_computation.12 | async-start | bytes 143360 | tf_op jit(solution)/shard_map/psum | solution.py:360
  348.9 217.5 %copy-start.5 = (bf16[3,196,512]{2,1,0:T(8,128)(2,1)S(1)}, bf16[3,196,512]{2,1,0:T(8,128)(2,1)}, u32[]{:S(2)}) copy-start(bf16[3,196,512]{2,1,0:T(8,128)(2,1)} %get-tuple-element.48.up) | copy-start | bytes 1806340
  348.9 217.5 %copy-start.6 = (bf16[3,196,512]{2,1,0:T(8,128)(2,1)S(1)}, bf16[3,196,512]{2,1,0:T(8,128)(2,1)}, u32[]{:S(2)}) copy-start(bf16[3,196,512]{2,1,0:T(8,128)(2,1)} %get-tuple-element.52) | copy-start | bytes 1806340
  563.1 1.5 collective-permute-start.2
  563.9 186.8 %all-gather.25.cloned.1.call-start = ((), (), s32[]{:S(2)}) async-start(), calls=%async_computation.11 | async-start | bytes 3538944 | tf_op jit(solution)/shard_map/all_gather | solution.py:382
  567.3 123.9 %collective-permute-start.1 = (bf16[3,196,512]{2,1,0:T(8,128)(2,1)}, bf16[3,196,512]{2,1,0:T(8,128)(2,1)}, u32[]{:S(2)}, u32[]{:S(2)}) collective-permute-start(bf16[3,196,512]{2,1,0:T(8,128)(2,1)} %broadcast_select_fusion.2), channel_id=1, source_target_pairs={{0,16},{16,0},{1,17},{17,1},{2,18},{18,2},{3,19},{19,3},{4,20},{20... | collective-permute-start | bytes 1806344 | tf_op jit(solution)/shard_map/ppermute | solution.py:261
  568.3 125.2 %collective-permute-start = (bf16[3,196,512]{2,1,0:T(8,128)(2,1)}, bf16[3,196,512]{2,1,0:T(8,128)(2,1)S(1)}, u32[]{:S(2)}, u32[]{:S(2)}) collective-permute-start(bf16[3,196,512]{2,1,0:T(8,128)(2,1)} %broadcast_select_fusion.6), channel_id=1, source_target_pairs={{0,16},{16,0},{1,17},{17,1},{2,18},{18,2},{3,19},{19,3},{4,20},{20... | collective-permute-start | bytes 1806344 | tf_op jit(solution)/shard_map/ppermute | solution.py:261
  (24 other events, 61.8 us)
Sparse Core Ops, SparseCore 0:
  9.6 29.8 all-gather.10
  41.1 33.1 all-gather.16
  75.8 33.1 all-gather.20
  110.3 9.0 all-gather.14
  120.8 13.2 all-gather.12
  135.5 14.8 all-gather.18
  152.0 14.8 all-gather.22
  326.5 115.4 reduce-scatter.2
  448.6 113.4 reduce-scatter.4
  568.1 117.3 all-reduce.7
  688.2 62.3 all-gather.24
